TPU v7x, 512 devices: a whole 4x8x8 slice. The times are simulated.
512 devices in a mesh: band: 16 (over z, core), tile: 32 (over y, x).
Axes of the slice: x: 4, y: 8, z: 8, core: 2. Of those that a mesh axis runs over, the one named last changes fastest.
Arguments:
- sources: bfloat16 [524288, 256], P(('band', 'tile')), may hold values from -6 to 6
- observed: bfloat16 [8192, 256], P('tile'), may hold values from -6 to 6
- v_factors: bfloat16 [8, 96, 524288], P(None, None, ('band', 'tile')), may hold values from -0.1875 to 0.1875
- u_factors: bfloat16 [512, 96, 8192], P('band', None, 'tile'), may hold values from -0.03125 to 0.03125
- tile_ranks: int32 [8, 512], P(None, ('band', 'tile')), may hold values from 32 to 96
- v_exponents: int32 [8, 512], P(None, ('band', 'tile')), may hold values from -1 to 1
- u_exponents: int32 [8, 512], P(None, ('band', 'tile')), may hold values from -1 to 1
Outputs:
- residual: float32 [8192, 256], P('tile', 'band')
- gradient: bfloat16 [524288, 256], P(('band', 'tile'))
All inputs are finite; a program needn't handle non-finite values.
Results may differ from a plain program's by a relative error of at most 0.012.
Values may be sent and summed in bfloat16 or wider, within the bound.
A program may use at most 64 MiB of HBM per device.

v0:
```python
import jax
import jax.numpy as jnp
from jax import lax
from jax.sharding import PartitionSpec as P


def local(sources, observed, v_factors, u_factors, tile_ranks, v_exponents, u_exponents):
    tile_count = lax.axis_size("tile")
    band_count = lax.axis_size("band")
    row_tiles = v_factors.shape[0]
    rank_max = v_factors.shape[1]
    slices_per = tile_count // row_tiles
    rank_index = jnp.arange(rank_max, dtype=jnp.int32)
    weight = (rank_index[None, :] < tile_ranks).astype(jnp.float32)
    weight = weight * jnp.exp2((v_exponents + u_exponents).astype(jnp.float32))
    products = jnp.einsum("ikb,bs->iks", v_factors, sources, preferred_element_type=jnp.float32)
    pieces = (products * weight[:, :, None]).astype(jnp.bfloat16)
    outgoing = jnp.repeat(pieces, slices_per, axis=0)
    incoming = lax.all_to_all(outgoing, "tile", split_axis=0, concat_axis=0, tiled=True)
    partial_value = jnp.einsum(
        "ukh,uks->hs", u_factors, incoming, preferred_element_type=jnp.float32
    )
    col_width = observed.shape[1] // band_count
    offset = lax.axis_index("band") * col_width
    totals = lax.psum(partial_value, "band")
    full_rows = totals - observed.astype(jnp.float32)
    residual = lax.dynamic_slice_in_dim(full_rows, offset, col_width, 1)
    residual_rows = full_rows.astype(jnp.bfloat16)
    adjoint_part = jnp.einsum(
        "ukh,hs->uks", u_factors, residual_rows, preferred_element_type=jnp.float32
    )
    returned = lax.all_to_all(
        adjoint_part.astype(jnp.bfloat16), "tile", split_axis=0, concat_axis=0, tiled=True
    )
    summed = (
        returned.astype(jnp.float32)
        .reshape(row_tiles, slices_per, rank_max, returned.shape[2])
        .sum(axis=1)
    )
    adjoint = (summed * weight[:, :, None]).astype(jnp.bfloat16)
    gradient = jnp.einsum("ikb,iks->bs", v_factors, adjoint, preferred_element_type=jnp.float32)
    return (residual, gradient.astype(jnp.bfloat16))


def solution(mesh):
    in_specs = (
        P(("band", "tile"), None),
        P("tile", None),
        P(None, None, ("band", "tile")),
        P("band", None, "tile"),
        P(None, ("band", "tile")),
        P(None, ("band", "tile")),
        P(None, ("band", "tile")),
    )
    out_specs = (P("tile", "band"), P(("band", "tile"), None))
    return jax.shard_map(local, mesh=mesh, in_specs=in_specs, out_specs=out_specs, check_vma=False)
```

profile of v0, /device:TPU:4, one launch (start us, length us, event | category | flops | bytes accessed | tf_op | source)
XLA Modules:
  0.0 238.3 jit_solution(13547615035790127038)
XLA Ops:
  7.2 0.0 copy-start
  7.2 0.0 all-reduce.2.cloned.1.call-start
  7.2 0.8 exponential_bitcast_fusion
  8.0 0.7 fusion.8
  8.7 2.1 fusion.2
  10.8 0.2 broadcast_in_dim.2
  11.0 49.3 %all_to_all.10 = bf16[32,96,256]{2,1,0:T(8,128)(2,1)S(1)} all-to-all(bf16[32,96,256]{2,1,0:T(8,128)(2,1)S(1)} %bitcast.32), channel_id=1, replica_groups=mesh['band'=16,'tile'=32] {'tile'}, dimensions={0} | all-to-all | bytes 3145728 | tf_op jit(solution)/shard_map/all_to_all | solution.py:19
  60.3 0.0 copy-done
  60.3 0.0 copy-start.1
  60.3 1.3 convolution_bitcast_fusion.1
  61.7 0.0 all-reduce.2.cloned.1.call-update
  61.7 0.0 copy-done.1
  61.7 0.1 copy.9
  61.8 114.5 %all-reduce.2.cloned.1.call-done = f32[256,256]{0,1:T(8,128)} async-done(((f32[256,256]{0,1:T(8,128)}), f32[256,256]{0,1:T(8,128)}) %all-reduce.2.cloned.1.call-update) | async-done | bytes 262160 | tf_op jit(solution)/shard_map/psum | solution.py:25
  176.3 1.0 convert_subtract_fusion
  177.3 1.8 fusion
  179.1 9.9 %all-to-all-start.1 = ((bf16[32,96,256]{2,1,0:T(8,128)(2,1)}), bf16[32,96,256]{2,1,0:T(8,128)(2,1)S(1)}, u32[]{:S(2)}, u32[]{:S(2)}) async-start(bf16[32,96,256]{2,1,0:T(8,128)(2,1)} %fusion), calls=%async_computation.1 | async-start | bytes 3145728 | tf_op jit(solution)/shard_map/all_to_all | solution.py:32
  189.0 0.6 constant_dynamic-slice_fusion
  189.6 38.7 %all-to-all-done.1 = bf16[32,96,256]{2,1,0:T(8,128)(2,1)S(1)} async-done(((bf16[32,96,256]{2,1,0:T(8,128)(2,1)}), bf16[32,96,256]{2,1,0:T(8,128)(2,1)S(1)}, u32[]{:S(2)}, u32[]{:S(2)}) %all-to-all-start.1) | async-done | bytes 1572896 | tf_op jit(solution)/shard_map/all_to_all | solution.py:32
  228.3 0.0 copy-start.2
  228.3 0.2 convert_reduce_fusion
  228.5 1.2 copy-done.2
  229.7 0.7 fusion.3
  230.4 1.0 copy.11
Async XLA Ops:
  7.2 53.2 %copy-start = (bf16[32,96,256]{2,1,0:T(8,128)(2,1)S(1)}, bf16[32,96,256]{2,1,0:T(8,128)(2,1)}, u32[]{:S(2)}) copy-start(bf16[32,96,256]{2,1,0:T(8,128)(2,1)} %param.10) | copy-start | bytes 4718596
  7.2 169.2 %all-reduce.2.cloned.1.call-start = ((), (), s32[]{:S(2)}) async-start(), calls=%async_computation.2 | async-start | bytes 524288 | tf_op jit(solution)/shard_map/psum | solution.py:25
  60.3 1.3 copy-start.1
  179.1 49.2 %all-to-all-start.1 = ((bf16[32,96,256]{2,1,0:T(8,128)(2,1)}), bf16[32,96,256]{2,1,0:T(8,128)(2,1)S(1)}, u32[]{:S(2)}, u32[]{:S(2)}) async-start(bf16[32,96,256]{2,1,0:T(8,128)(2,1)} %fusion), calls=%async_computation.1 | async-start | bytes 3145728 | tf_op jit(solution)/shard_map/all_to_all | solution.py:32
  228.3 1.4 copy-start.2
Sparse Core Ops, SparseCore 0:
  61.8 114.4 all-reduce.1
where the time goes:
time: 239 us; the launch traced here: 238 us
  waiting for transfers between devices  153 us (64%)
  blocking collectives  49.3 us (21%)
  between operations  14.1 us (6%)
  starting transfers between devices  9.9 us (4%)
  matrix products  5.87 us (2%)
  local copies, waits for them, and re-layouts  3.08 us (1%)
  other arithmetic  2.71 us (1%)
    psum x1, waiting for transfers between devices, local(): totals = lax.psum(partial_value, 'band')  115 us
    all_to_all x1, blocking collectives, local(): lax.all_to_all(outgoing, 'tile', split_axis=0, concat_axis=0, tiled=True)  49.3 us
    all_to_all x1, waiting for transfers between devices, local(): lax.all_to_all(adjoint_part.astype(jnp.bfloat16), 'tile', split_axis=0, c...  38.7 us
    all_to_all x1, starting transfers between devices, local(): lax.all_to_all(adjoint_part.astype(jnp.bfloat16), 'tile', split_axis=0, c...  9.86 us
  transfers between devices with their start and end apart: 2, of which 2 were waited for; matrix products, arithmetic and copies ran while one was open for 0% of the time, Pallas kernels for 0%

commit v1 on v0

--- a/solution.py
+++ b/solution.py
@@ -22,7 +22,7 @@
     )
     col_width = observed.shape[1] // band_count
     offset = lax.axis_index("band") * col_width
-    totals = lax.psum(partial_value, "band")
+    totals = jnp.sum(lax.all_gather(partial_value, "band"), axis=0)
     full_rows = totals - observed.astype(jnp.float32)
     residual = lax.dynamic_slice_in_dim(full_rows, offset, col_width, 1)
     residual_rows = full_rows.astype(jnp.bfloat16)

time: 239 us -> 174 us (0.73)
  waiting for transfers between devices: 153 us -> 84.8 us
  local copies, waits for them, and re-layouts: 3.08 us -> 7 us
    psum x1 -> x0, waiting for transfers between devices: 115 us -> none  [local(): totals = lax.psum(partial_value, 'band')]
    all_gather x0 -> x1, waiting for transfers between devices: none -> 45.7 us  [local(): totals = jnp.sum(lax.all_gather(partial_value, 'band'), axis=0)]
    unnamed x8 -> x9, local copies, waits for them, and re-layouts: 2.29 us -> 6.21 us
where the time goes in v1:
time: 174 us
  waiting for transfers between devices  84.8 us (49%)
  blocking collectives  49.3 us (28%)
  between operations  14.1 us (8%)
  starting transfers between devices  9.9 us (6%)
  local copies, waits for them, and re-layouts  7 us (4%)
  matrix products  5.87 us (3%)
  other arithmetic  2.82 us (2%)
    all_to_all x1, blocking collectives, local(): lax.all_to_all(outgoing, 'tile', split_axis=0, concat_axis=0, tiled=True)  49.3 us
    all_gather x1, waiting for transfers between devices, local(): totals = jnp.sum(lax.all_gather(partial_value, 'band'), axis=0)  45.7 us
    all_to_all x1, waiting for transfers between devices, local(): lax.all_to_all(adjoint_part.astype(jnp.bfloat16), 'tile', split_axis=0, c...  39.1 us
    all_to_all x1, starting transfers between devices, local(): lax.all_to_all(adjoint_part.astype(jnp.bfloat16), 'tile', split_axis=0, c...  9.86 us
    unnamed x9, local copies, waits for them, and re-layouts  6.21 us
  transfers between devices with their start and end apart: 2, of which 2 were waited for; matrix products, arithmetic and copies ran while one was open for 0% of the time, Pallas kernels for 0%

profile of v1, /device:TPU:4, one launch (start us, length us, event | category | flops | bytes accessed | tf_op | source)
XLA Modules:
  0.0 173.8 jit_solution(7070174367743881926)
XLA Ops:
  7.2 0.0 copy-start
  7.2 0.0 all-gather.3.cloned.1.call-start
  7.2 0.8 exponential_bitcast_fusion
  8.0 0.7 fusion.8
  8.7 2.1 %fusion.2 = bf16[8,96,256]{2,1,0:T(8,128)(2,1)S(1)} fusion(bf16[8,96,1024]{2,1,0:T(8,128)(2,1)} %param.9, bf16[1024,256]{1,0:T(8,128)(2,1)} %param.7, f32[8,96]{1,0:T(8,128)S(1)} %fusion.8), kind=kOutput, calls=%fused_computation.7 | convolution fusion | flops 403046400 | bytes 2493440 | tf_op jit(solution)/shard_map/ikb,bs->iks/dot_general | solution.py:16
  10.8 0.2 broadcast_in_dim.2
  11.0 49.3 %all_to_all.10 = bf16[32,96,256]{2,1,0:T(8,128)(2,1)S(1)} all-to-all(bf16[32,96,256]{2,1,0:T(8,128)(2,1)S(1)} %bitcast.37), channel_id=1, replica_groups=mesh['band'=16,'tile'=32] {'tile'}, dimensions={0} | all-to-all | bytes 3145728 | tf_op jit(solution)/shard_map/all_to_all | solution.py:19
  60.3 0.0 copy-done
  60.3 0.0 copy-start.1
  60.3 1.3 convolution_bitcast_fusion.1
  61.7 0.0 all-gather.3.cloned.1.call-update
  61.7 0.0 copy-done.1
  61.7 0.1 copy.9
  61.8 45.7 %all-gather.3.cloned.1.call-done = f32[4096,256]{0,1:T(8,128)} async-done(((f32[256,256]{0,1:T(8,128)}), f32[4096,256]{0,1:T(8,128)}) %all-gather.3.cloned.1.call-update) | async-done | bytes 4194320 | tf_op jit(solution)/shard_map/all_gather | solution.py:25
  107.5 3.9 %copy.14 = f32[32,8,16,256]{3,2,1,0:T(8,128)S(1)} copy(f32[32,8,16,256]{3,1,2,0:T(8,128)} %bitcast.38) | data formatting | bytes 8388608
  111.4 1.0 bitcast_reduce_fusion
  112.5 1.8 %fusion = bf16[32,96,256]{2,1,0:T(8,128)(2,1)} fusion(bf16[32,96,256]{2,1,0:T(8,128)(2,1)S(1)} %copy-done, f32[256,256]{0,1:T(8,128)S(1)} %convert_subtract_fusion), kind=kOutput, calls=%fused_computation.3 | convolution fusion | flops 403505152 | bytes 3407872 | tf_op jit(solution)/shard_map/ukh,hs->uks/dot_general | solution.py:29
  114.3 9.9 %all-to-all-start.1 = ((bf16[32,96,256]{2,1,0:T(8,128)(2,1)}), bf16[32,96,256]{2,1,0:T(8,128)(2,1)S(1)}, u32[]{:S(2)}, u32[]{:S(2)}) async-start(bf16[32,96,256]{2,1,0:T(8,128)(2,1)} %fusion), calls=%async_computation.1 | async-start | bytes 3145728 | tf_op jit(solution)/shard_map/all_to_all | solution.py:32
  124.2 0.6 constant_dynamic-slice_fusion
  124.8 39.1 %all-to-all-done.1 = bf16[32,96,256]{2,1,0:T(8,128)(2,1)S(1)} async-done(((bf16[32,96,256]{2,1,0:T(8,128)(2,1)}), bf16[32,96,256]{2,1,0:T(8,128)(2,1)S(1)}, u32[]{:S(2)}, u32[]{:S(2)}) %all-to-all-start.1) | async-done | bytes 1572896 | tf_op jit(solution)/shard_map/all_to_all | solution.py:32
  163.9 0.0 copy-start.2
  163.9 0.2 convert_reduce_fusion
  164.1 1.2 copy-done.2
  165.3 0.7 fusion.3
  166.0 1.0 copy.11
  (1 shorter events, 0.0 us)
Async XLA Ops:
  7.2 53.2 %copy-start = (bf16[32,96,256]{2,1,0:T(8,128)(2,1)S(1)}, bf16[32,96,256]{2,1,0:T(8,128)(2,1)}, u32[]{:S(2)}) copy-start(bf16[32,96,256]{2,1,0:T(8,128)(2,1)} %param.10) | copy-start | bytes 4718596
  7.2 100.3 %all-gather.3.cloned.1.call-start = ((), (), s32[]{:S(2)}) async-start(), calls=%async_computation.2 | async-start | bytes 4456448 | tf_op jit(solution)/shard_map/all_gather | solution.py:25
  60.3 1.3 copy-start.1
  114.3 49.6 %all-to-all-start.1 = ((bf16[32,96,256]{2,1,0:T(8,128)(2,1)}), bf16[32,96,256]{2,1,0:T(8,128)(2,1)S(1)}, u32[]{:S(2)}, u32[]{:S(2)}) async-start(bf16[32,96,256]{2,1,0:T(8,128)(2,1)} %fusion), calls=%async_computation.1 | async-start | bytes 3145728 | tf_op jit(solution)/shard_map/all_to_all | solution.py:32
  163.9 1.4 copy-start.2
Sparse Core Ops, SparseCore 0:
  61.8 45.6 all-gather.2
